TPU v7x, 32 devices: a whole 2x2x4 slice. The times are simulated.
32 devices in a mesh: grp: 4 (over z), seq: 8 (over y, x, core).
Axes of the slice: x: 2, y: 2, z: 4, core: 2. Of those that a mesh axis runs over, the one named last changes fastest.
Arguments:
- queries: bfloat16 [4096, 6144], P(('grp', 'seq')), may hold values from -64 to 64
- keys_values: bfloat16 [4096, 768], P(('grp', 'seq')), may hold values from -6 to 6
- selection: int32 [64, 32], P(('grp', 'seq')), may hold values from -1 to 63, as said below
- gate_logits: bfloat16 [3, 4096, 32], P(None, ('grp', 'seq')), may hold values from -6 to 6
- pos_weight: bfloat16 [64, 384], replicated, may hold values from -0.75 to 0.75
- compress_weight: bfloat16 [384, 384], replicated, may hold values from -0.3125 to 0.3125
Outputs:
- attended: bfloat16 [4096, 6144], P(('grp', 'seq'))
Inputs may be any that keep to these rules, and one draw needn't show every extreme that they name: `selection`: A run is the 2 rows of one device; a segment is 16 consecutive rows. Row r lists, for each group, 16 distinct block numbers no greater than r, or -1 for unused entries. Within one group, the rows of a run list from each earlier segment exactly one block, and it lies in the run at the same place of that segment; from any other run of their own segment they list at most one block.
All inputs are finite; a program needn't handle non-finite values.
Results may differ from a plain program's by a relative error of at most 0.0055.
Values may be sent and summed in bfloat16 or wider, within the bound.
A program may use at most 128 MiB of HBM per device.

v0:
```python
import math
import jax
import jax.numpy as jnp
from jax import lax
from jax.sharding import PartitionSpec as P

HEAD_DIM = 192
GROUPS = 2
GROUP_HEADS = 16
HEADS = 32
BLOCK = 64
TOP = 16
CAP = 2
WINDOW = 128
NEG_FILL = -1e30


def from_behind(block, axis, distance):
    devices = range(lax.axis_size(axis))
    route = [(i - distance, i) for i in devices if i - distance in devices]
    return lax.ppermute(block, axis, route)


def attend(query_block, key_block, allowed, with_sink):
    head_dim = query_block.shape[-1]
    score_scale = head_dim ** (-0.5)
    scores = (
        jnp.einsum(
            "btghd,bgnd->bghtn",
            query_block,
            key_block[..., :head_dim],
            preferred_element_type=jnp.float32,
        )
        * score_scale
    )
    allowed_wide = allowed[:, :, None]
    scores = jnp.where(allowed_wide, scores, NEG_FILL)
    top_score = jnp.max(scores, axis=-1, keepdims=True)
    if with_sink:
        top_score = jnp.maximum(top_score, 0.0)
    weights = jnp.where(allowed_wide, jnp.exp(scores - top_score), 0.0)
    denominator = jnp.sum(weights, axis=-1, keepdims=True)
    if with_sink:
        denominator = denominator + jnp.exp(-top_score)
    rounded = weights.astype(jnp.bfloat16)
    blended = (
        jnp.einsum(
            "bghtn,bgnd->bghtd",
            rounded,
            key_block[..., head_dim:],
            preferred_element_type=jnp.float32,
        )
        / denominator
    )
    return jnp.transpose(blended, (0, 3, 1, 2, 4))


def by_heads(query_block, key_block, allowed, with_sink):
    head_count = query_block.shape[3]
    slab_width = math.gcd(4, head_count)

    def head_slab(slab_index):
        query_slab = lax.dynamic_slice_in_dim(query_block, slab_index * slab_width, slab_width, 3)
        return attend(query_slab, key_block, allowed, with_sink)

    stacked = lax.map(head_slab, jnp.arange(head_count // slab_width, dtype=jnp.int32))
    stacked = jnp.moveaxis(stacked, 0, 3)
    return stacked.reshape(stacked.shape[:3] + (head_count, stacked.shape[-1]))


def compress_blocks(keys_values, pos_weight, compress_weight):
    block_count = keys_values.shape[0] // BLOCK
    grouped = keys_values.reshape(block_count, BLOCK, GROUPS, 2 * HEAD_DIM).astype(jnp.float32)
    pooled = jnp.sum(grouped * pos_weight.astype(jnp.float32)[None, :, None, :], axis=1).astype(
        jnp.bfloat16
    )
    mapped = jnp.dot(
        pooled.reshape(block_count * GROUPS, 2 * HEAD_DIM),
        compress_weight,
        preferred_element_type=jnp.float32,
    )
    return mapped.astype(jnp.bfloat16).reshape(block_count, GROUPS, 2 * HEAD_DIM)


def plan_requests(unit_of, key_of, wanted, unit_count, key_count):
    hits = (
        wanted[:, None, None]
        & (unit_of[:, None, None] == jnp.arange(unit_count, dtype=jnp.int32)[None, :, None])
        & (key_of[:, None, None] == jnp.arange(key_count, dtype=jnp.int32)[None, None, :])
    )
    present = jnp.any(hits, axis=0)
    ordinal = jnp.cumsum(present.astype(jnp.int32), axis=1) - 1
    slot_of = jnp.sum(jnp.where(hits, ordinal[None], 0), axis=(1, 2))
    matches = present[:, :, None] & (
        ordinal[:, :, None] == jnp.arange(CAP, dtype=jnp.int32)[None, None, :]
    )
    requests = (
        jnp.sum(
            jnp.where(matches, jnp.arange(key_count, dtype=jnp.int32)[None, :, None] + 1, 0), axis=1
        )
        - 1
    )
    return (slot_of, requests)


def shards(queries, keys_values, selection, gate_logits, pos_weight, compress_weight):
    grp_index = lax.axis_index("grp")
    seq_index = lax.axis_index("seq")
    grp_count = lax.axis_size("grp")
    seq_count = lax.axis_size("seq")
    tok_count = queries.shape[0]
    dev_blocks = tok_count // BLOCK
    seg_tokens = tok_count * seq_count
    seg_blocks = seg_tokens // BLOCK
    all_blocks = seg_blocks * grp_count
    key_count = GROUPS * dev_blocks
    first_pos = (grp_index * seq_count + seq_index) * tok_count
    positions = first_pos + jnp.arange(tok_count, dtype=jnp.int32)
    local_view = keys_values.reshape(dev_blocks, BLOCK, GROUPS, 2 * HEAD_DIM)
    local_summary = jnp.transpose(
        compress_blocks(keys_values, pos_weight, compress_weight), (1, 0, 2)
    )
    summaries = lax.all_gather(local_summary, ("grp", "seq"), axis=1, tiled=True)
    picked = selection.reshape(dev_blocks, GROUPS, TOP)
    group_ids = jnp.broadcast_to(jnp.arange(GROUPS, dtype=jnp.int32)[None, :, None], picked.shape)
    flat_groups = group_ids.reshape(-1)
    flat_picks = picked.reshape(-1)
    clipped_flat = jnp.maximum(flat_picks, 0)
    segment_of = clipped_flat // seg_blocks
    key_of = flat_groups * dev_blocks + clipped_flat % dev_blocks
    wanted = (flat_picks >= 0) & (segment_of != grp_index)
    slot_of, requests = plan_requests(segment_of, key_of, wanted, grp_count, key_count)
    asked_clipped = jnp.maximum(
        lax.all_to_all(requests, "grp", split_axis=0, concat_axis=0, tiled=True), 0
    )
    received = lax.all_to_all(
        local_view[asked_clipped % dev_blocks, :, asked_clipped // dev_blocks, :],
        "grp",
        split_axis=0,
        concat_axis=0,
        tiled=True,
    )
    picks_clipped = jnp.maximum(picked, 0)
    pick_segment = picks_clipped // seg_blocks
    from_remote = received[pick_segment, slot_of.reshape(picked.shape)]
    segment = lax.all_gather(keys_values, "seq", axis=0, tiled=True)
    earlier_tail = from_behind(segment[seg_tokens - WINDOW :], "grp", 1)
    segment_view = segment.reshape(seg_blocks, BLOCK, GROUPS, 2 * HEAD_DIM)
    from_segment = segment_view[picks_clipped % seg_blocks, :, group_ids, :]
    start_row = jnp.maximum(seq_index * tok_count - WINDOW, 0)
    inside = lax.dynamic_slice_in_dim(segment, start_row, WINDOW, 0)
    before = jnp.where(seq_index == 0, earlier_tail, inside)
    own_rows = (pick_segment == grp_index)[..., None, None]
    chosen = jnp.where(own_rows, from_segment, from_remote).reshape(
        dev_blocks, GROUPS, TOP * BLOCK, 2 * HEAD_DIM
    )
    key_positions = (picks_clipped[..., None] * BLOCK + jnp.arange(BLOCK, dtype=jnp.int32)).reshape(
        dev_blocks, GROUPS, TOP * BLOCK
    )
    live_keys = jnp.repeat(picked >= 0, BLOCK, axis=2)
    block_positions = positions.reshape(dev_blocks, BLOCK)
    allowed_sel = live_keys[:, :, None, :] & (
        key_positions[:, :, None, :] <= block_positions[:, None, :, None]
    )
    query_blocks = queries.reshape(dev_blocks, BLOCK, GROUPS, GROUP_HEADS, HEAD_DIM)
    selected_branch = by_heads(query_blocks, chosen, allowed_sel, False).reshape(
        tok_count, GROUPS, GROUP_HEADS, HEAD_DIM
    )
    query_whole = queries.reshape(1, tok_count, GROUPS, GROUP_HEADS, HEAD_DIM)
    block_ends = jnp.arange(all_blocks, dtype=jnp.int32) * BLOCK + BLOCK - 1
    allowed_comp = (block_ends[None, :] <= positions[:, None])[None, None]
    compressed_branch = by_heads(query_whole, summaries[None], allowed_comp, True)[0]
    nearby = jnp.concatenate([before, keys_values], axis=0).reshape(
        WINDOW + tok_count, GROUPS, 2 * HEAD_DIM
    )
    nearby = jnp.transpose(nearby, (1, 0, 2))[None]
    near_positions = first_pos - WINDOW + jnp.arange(WINDOW + tok_count, dtype=jnp.int32)
    allowed_win = (
        (near_positions[None, :] <= positions[:, None])
        & (near_positions[None, :] > positions[:, None] - WINDOW)
        & (near_positions[None, :] >= 0)
    )[None, None]
    window_branch = by_heads(query_whole, nearby, allowed_win, False)[0]
    gate_values = jax.nn.sigmoid(gate_logits.astype(jnp.float32)).reshape(
        3, tok_count, GROUPS, GROUP_HEADS, 1
    )
    attended = (
        gate_values[0] * compressed_branch
        + gate_values[1] * selected_branch
        + gate_values[2] * window_branch
    )
    return attended.reshape(tok_count, HEADS * HEAD_DIM).astype(jnp.bfloat16)


def solution(mesh):
    in_specs = (
        P(("grp", "seq"), None),
        P(("grp", "seq"), None),
        P(("grp", "seq"), None),
        P(None, ("grp", "seq"), None),
        P(),
        P(),
    )
    out_specs = P(("grp", "seq"), None)
    return jax.shard_map(shards, mesh=mesh, in_specs=in_specs, out_specs=out_specs, check_vma=False)
```

profile of v0, /device:TPU:0, one launch (start us, length us, event | category | flops | bytes accessed | tf_op | source)
XLA Modules:
  0.0 216.7 jit_solution(13625318544058351301)
XLA Ops:
  10.9 6.3 %all-to-all-start = ((s32[4,1,2]{2,1,0:T(1,128)}), s32[4,1,2]{2,1,0:T(1,128)}, u32[]{:S(2)}, u32[]{:S(2)}) async-start(s32[4,1,2]{2,1,0:T(1,128)} %copy.101), calls=%async_computation | async-start | bytes 4096 | tf_op jit(solution)/shard_map/all_to_all | solution.py:134
  18.9 2.6 %copy.97 = bf16[128,6144]{0,1:T(8,128)(2,1)} copy(bf16[128,6144]{1,0:T(8,128)(2,1)} %param.12) | data formatting | bytes 3145728 | tf_op args[0]
  22.0 42.4 %all_gather.6 = bf16[2,64,384]{2,0,1:T(2,128)(2,1)S(1)} all-gather(bf16[2,2,384]{2,0,1:T(2,128)(2,1)S(1)} %bitcast.261), channel_id=1, replica_groups=mesh['grp'=4,'seq'=8] {'grp','seq'}, dimensions={1}, use_global_device_ids=true | all-gather | bytes 101376 | tf_op jit(solution)/shard_map/all_gather | solution.py:123
  65.3 14.9 %while.33 = (s32[]{:T(128)}, f32[4,1,128,2,4,192]{2,5,4,0,3,1:T(8,128)S(1)}, s32[4]{0:T(128)}, bf16[1,128,2,16,192]{1,4,3,2,0:T(8,128)(2,1)}, bf16[1,2,64,384]{3...) while((s32[]{:T(128)}, ...), condition=%wide.region_4.5_spmd.clone, body=%wide.region_1.4_spmd.clone.sunk | while | flops 51128324 | bytes 2171823 | solution.py:66
  87.3 2.3 %gather_fusion.1 = bf16[8,64,384]{2,1,0:T(8,128)(2,1)} fusion(bf16[2,64,2,384]{3,1,2,0:T(8,128)(2,1)} %copy.106, s32[8]{0:T(128)S(1)} %reshape.547), kind=kCustom, calls=%fused_computation.1 | custom fusion | bytes 786496 | tf_op jit(solution)/shard_map/gather | solution.py:137
  89.6 3.5 %all-to-all-start.1 = ((bf16[4,2,64,384]{3,2,1,0:T(8,128)(2,1)}), bf16[4,2,64,384]{3,2,1,0:T(8,128)(2,1)S(1)}, u32[]{:S(2)}, u32[]{:S(2)}) async-start(bf16[4,2,64,384]{3,2,1,0:T(8,128)(2,1)} %bitcast.255), calls=%async_computation.1 | async-start | bytes 786432 | tf_op jit(solution)/shard_map/all_to_all | solution.py:136
  93.8 4.7 %reshape.537 = bf16[2,64,2,16,192]{4,3,2,1,0:T(8,128)(2,1)} reshape(bf16[128,6144]{1,0:T(8,128)(2,1)} %param.12) | data formatting | bytes 3145728 | tf_op jit(solution)/shard_map/reshape | solution.py:165
  99.1 6.4 %all-to-all-done.1 = bf16[4,2,64,384]{3,2,1,0:T(8,128)(2,1)S(1)} async-done(((bf16[4,2,64,384]{3,2,1,0:T(8,128)(2,1)}), bf16[4,2,64,384]{3,2,1,0:T(8,128)(2,1)S(1)}, u32[]{:S(2)}, u32[]{:S(2)}) %all-to-all-start.1) | async-done | bytes 393248 | tf_op jit(solution)/shard_map/all_to_all | solution.py:136
  105.5 2.7 %gather_fusion.2 = bf16[64,64,384]{2,1,0:T(8,128)(2,1)} fusion(bf16[4,2,64,384]{3,2,1,0:T(8,128)(2,1)S(1)} %all-to-all-done.1, s32[64]{0:T(128)S(1)} %reshape.553), kind=kCustom, calls=%fused_computation.2 | custom fusion | bytes 6291968 | tf_op jit(solution)/shard_map/gather | solution.py:145
  108.2 3.4 %reshape.538 = bf16[16,64,2,384]{3,2,1,0:T(2,128)(2,1)S(1)} reshape(bf16[1024,768]{1,0:T(8,128)(2,1)} %all-gather.2.cloned.1.call-done) | data formatting | bytes 3145728 | tf_op jit(solution)/shard_map/reshape | solution.py:148
  111.9 2.7 %gather_fusion = bf16[64,64,384]{2,1,0:T(8,128)(2,1)} fusion(bf16[16,64,2,384]{3,1,2,0:T(8,128)(2,1)S(1)} %copy.100, s32[64]{0:T(128)S(1)} %reshape.541), kind=kCustom, calls=%fused_computation | custom fusion | bytes 6291968 | tf_op jit(solution)/shard_map/gather | solution.py:149
  114.6 4.4 %broadcast_select_fusion = bf16[2,2,1024,384]{3,2,1,0:T(8,128)(2,1)} fusion(bf16[2,2,1024,384]{3,2,1,0:T(8,128)(2,1)} %bitcast.253, bf16[2,2,1024,384]{3,2,1,0:T(8,128)(2,1)} %bitcast.252, pred[2,2,1024]{2,1,0:T(4,128)(4,1)S(1)} %broadcast_in_dim.161), kind=kLoop, calls=%fused_computation.84 | loop fusion | flops 1572864 | bytes 9441280 | tf_op jit(solution)/shard_map/jit(_where)/select_n | solution.py:154
  119.0 3.2 %copy.108 = bf16[2,2,1024,384]{2,3,1,0:T(8,128)(2,1)S(1)} copy(bf16[2,2,1024,384]{3,2,1,0:T(8,128)(2,1)} %broadcast_select_fusion) | data formatting | bytes 6291456
  125.9 30.6 %while.34 = (s32[]{:T(128)}, f32[4,2,64,2,4,192]{5,2,4,3,1,0:T(8,128)}, s32[4]{0:T(128)S(1)}, bf16[2,64,2,16,192]{4,3,2,1,0:T(8,128)(2,1)}, bf16[2,2,1024,384]{2...) while((s32[]{:T(128)}, ...), condition=%wide.region_12.13_spmd.clone, body=%wide.region_9.12_spmd.clone.sunk | while | flops 814416896 | bytes 18646196 | solution.py:66
  129.6 2.1 fusion.132
  156.4 11.7 %copy.121 = f32[2,64,2,4,4,192]{1,0,5,4,3,2:T(2,128)} copy(f32[2,64,2,4,4,192]{5,1,4,2,0,3:T(8,128)} %bitcast.16) | data formatting | bytes 6291456 | tf_op jit(solution)/shard_map/reshape;reshape | solution.py:166
  168.1 5.8 %reshape.575 = f32[128,6144]{0,1:T(8,128)S(1)} reshape(f32[2,64,2,4,4,192]{1,0,5,4,3,2:T(2,128)} %copy.121) | data formatting | bytes 6291456 | tf_op jit(solution)/shard_map/reshape;reshape | solution.py:166
  180.7 21.9 %while.35 = (s32[]{:T(128)}, f32[4,1,128,2,4,192]{2,5,4,0,3,1:T(8,128)}, s32[4]{0:T(128)S(1)}, bf16[1,128,2,16,192]{1,4,3,2,0:T(8,128)(2,1)}, bf16[1,2,256,384]{...) while((s32[]{:T(128)}, ...), condition=%wide.region_16.17_spmd.clone, body=%wide.region_13.16_spmd.clone.sunk | while | flops 204011520 | bytes 4873147 | solution.py:66
  184.0 2.2 %fusion.138 = f32[4,1,128,2,4,192]{2,5,4,0,3,1:T(8,128)} fusion(f32[4,1,128,2,4,192]{2,5,4,0,3,1:T(8,128)} %get-tuple-element.488, s32[]{:T(128)} %get-tuple-element.487, f32[1,2,4,128,256]{4,3,2,1,0:T(8,128)S(1)} %get-tuple-element.472, f32[2,4,128]{2,1,0:T(4,128)S(1)} %get-tuple-element.473, pred[128,256]{1,0:T(8,128)(4,1)S(1)} %and_and_fusion.2, ...), kind=kOutput, calls=%fused_computation.60.clone.1 | convolution fusion | flops 101646336 | bytes 2073088 | tf_op jit(solution)/shard_map/while/body/eval_jaxpr/bghtn,bgnd->bghtd/dot_general | solution.py:47
  189.4 2.2 %fusion.138 = f32[4,1,128,2,4,192]{2,5,4,0,3,1:T(8,128)} fusion(f32[4,1,128,2,4,192]{2,5,4,0,3,1:T(8,128)} %get-tuple-element.488, s32[]{:T(128)} %get-tuple-element.487, f32[1,2,4,128,256]{4,3,2,1,0:T(8,128)S(1)} %get-tuple-element.472, f32[2,4,128]{2,1,0:T(4,128)S(1)} %get-tuple-element.473, pred[128,256]{1,0:T(8,128)(4,1)S(1)} %and_and_fusion.2, ...), kind=kOutput, calls=%fused_computation.60.clone.1 | convolution fusion | flops 101646336 | bytes 2073088 | tf_op jit(solution)/shard_map/while/body/eval_jaxpr/bghtn,bgnd->bghtd/dot_general | solution.py:47
  194.9 2.2 %fusion.138 = f32[4,1,128,2,4,192]{2,5,4,0,3,1:T(8,128)} fusion(f32[4,1,128,2,4,192]{2,5,4,0,3,1:T(8,128)} %get-tuple-element.488, s32[]{:T(128)} %get-tuple-element.487, f32[1,2,4,128,256]{4,3,2,1,0:T(8,128)S(1)} %get-tuple-element.472, f32[2,4,128]{2,1,0:T(4,128)S(1)} %get-tuple-element.473, pred[128,256]{1,0:T(8,128)(4,1)S(1)} %and_and_fusion.2, ...), kind=kOutput, calls=%fused_computation.60.clone.1 | convolution fusion | flops 101646336 | bytes 2073088 | tf_op jit(solution)/shard_map/while/body/eval_jaxpr/bghtn,bgnd->bghtd/dot_general | solution.py:47
  200.4 2.3 %fusion.138 = f32[4,1,128,2,4,192]{2,5,4,0,3,1:T(8,128)} fusion(f32[4,1,128,2,4,192]{2,5,4,0,3,1:T(8,128)} %get-tuple-element.488, s32[]{:T(128)} %get-tuple-element.487, f32[1,2,4,128,256]{4,3,2,1,0:T(8,128)S(1)} %get-tuple-element.472, f32[2,4,128]{2,1,0:T(4,128)S(1)} %get-tuple-element.473, pred[128,256]{1,0:T(8,128)(4,1)S(1)} %and_and_fusion.2, ...), kind=kOutput, calls=%fused_computation.60.clone.1 | convolution fusion | flops 101646336 | bytes 2073088 | tf_op jit(solution)/shard_map/while/body/eval_jaxpr/bghtn,bgnd->bghtd/dot_general | solution.py:47
  202.6 4.6 %fusion.84 = bf16[128,6144]{0,1:T(8,128)(2,1)} fusion(f32[4,1,128,2,4,192]{2,5,4,0,3,1:T(8,128)} %get-tuple-element.103, f32[4,1,128,2,4,192]{2,5,4,0,3,1:T(8,128)} %copy-done.1, f32[128,6144]{0,1:T(8,128)S(1)} %reshape.575, f32[128,2,16]{0,2,1:T(8,128)S(1)} %bitcast.259, f32[128,2,16]{0,2,1:T(8,128)S(1)} %bitcast.260, f32[128,2,16]{0,2,1:T(8,128)S(1)} %bitcast.258), kind=kLoop, calls=%fused_computation.80 | loop fusion | flops 4718592 | bytes 11059200 | tf_op jit(solution)/shard_map/convert_element_type | solution.py:192
  207.3 2.6 %copy.113 = bf16[128,6144]{1,0:T(8,128)(2,1)} copy(bf16[128,6144]{0,1:T(8,128)(2,1)} %fusion.84) | data formatting | bytes 3145728 | tf_op jit(solution)/shard_map/convert_element_type | solution.py:192
  (163 shorter events, 75.0 us)
Async XLA Ops:
  6.5 15.3 %copy-start = (bf16[384,384]{1,0:T(8,128)(2,1)S(1)}, bf16[384,384]{1,0:T(8,128)(2,1)}, u32[]{:S(2)}) copy-start(bf16[384,384]{1,0:T(8,128)(2,1)} %param.17) | copy-start | bytes 884740
  6.5 15.0 %copy-start.3 = (bf16[64,384]{1,0:T(8,128)(2,1)S(1)}, bf16[64,384]{1,0:T(8,128)(2,1)}, u32[]{:S(2)}) copy-start(bf16[64,384]{1,0:T(8,128)(2,1)} %param.16) | copy-start | bytes 147460
  9.1 8.1 %copy-start.7 = (pred[2,32]{1,0:T(4,128)(4,1)}, pred[2,32]{1,0:T(4,128)(4,1)S(1)}, u32[]{:S(2)}) copy-start(pred[2,32]{1,0:T(4,128)(4,1)S(1)} %get-tuple-element.310) | copy-start | bytes 196
  9.1 8.1 %copy-start.8 = (pred[2,32]{1,0:T(4,128)(4,1)}, pred[2,32]{1,0:T(4,128)(4,1)S(1)}, u32[]{:S(2)}) copy-start(pred[2,32]{1,0:T(4,128)(4,1)S(1)} %get-tuple-element.293) | copy-start | bytes 196
  9.5 0.5 copy-start.5
  9.5 12.5 %copy-start.6 = (pred[64,4]{0,1:T(4,128)(4,1)}, pred[64,4]{0,1:T(4,128)(4,1)S(1)}, u32[]{:S(2)}) copy-start(pred[64,4]{0,1:T(4,128)(4,1)S(1)} %get-tuple-element.312) | copy-start | bytes 772
  10.9 75.5 %all-to-all-start = ((s32[4,1,2]{2,1,0:T(1,128)}), s32[4,1,2]{2,1,0:T(1,128)}, u32[]{:S(2)}, u32[]{:S(2)}) async-start(s32[4,1,2]{2,1,0:T(1,128)} %copy.101), calls=%async_computation | async-start | bytes 4096 | tf_op jit(solution)/shard_map/all_to_all | solution.py:134
  17.2 91.0 %all-gather.2.cloned.1.call-start = ((), (), s32[]{:S(2)}) async-start(), calls=%async_computation.2 | async-start | bytes 1769472 | tf_op jit(solution)/shard_map/all_gather | solution.py:146
  18.9 45.5 %copy-start.2 = (bf16[2,64,2,384]{3,2,1,0:T(2,128)(2,1)}, bf16[2,64,2,384]{3,2,1,0:T(2,128)(2,1)S(1)}, u32[]{:S(2)}) copy-start(bf16[2,64,2,384]{3,2,1,0:T(2,128)(2,1)S(1)} %reshape.535) | copy-start | bytes 589828
  80.2 9.4 %copy-start.1 = (f32[4,1,128,2,4,192]{2,5,4,0,3,1:T(8,128)}, f32[4,1,128,2,4,192]{2,5,4,0,3,1:T(8,128)S(1)}, u32[]{:S(2)}) copy-start(f32[4,1,128,2,4,192]{2,5,4,0,3,1:T(8,128)S(1)} %get-tuple-element.101) | copy-start | bytes 9437188
  80.2 18.9 %copy-start.4 = (bf16[3,128,32]{1,2,0:T(8,128)(2,1)S(1)}, bf16[3,128,32]{1,2,0:T(8,128)(2,1)}, u32[]{:S(2)}) copy-start(bf16[3,128,32]{1,2,0:T(8,128)(2,1)} %param.15) | copy-start | bytes 73732
  89.6 15.9 %all-to-all-start.1 = ((bf16[4,2,64,384]{3,2,1,0:T(8,128)(2,1)}), bf16[4,2,64,384]{3,2,1,0:T(8,128)(2,1)S(1)}, u32[]{:S(2)}, u32[]{:S(2)}) async-start(bf16[4,2,64,384]{3,2,1,0:T(8,128)(2,1)} %bitcast.255), calls=%async_computation.1 | async-start | bytes 786432 | tf_op jit(solution)/shard_map/all_to_all | solution.py:136
  123.8 50.2 %collective-permute-start = (bf16[128,768]{1,0:T(8,128)(2,1)}, bf16[128,768]{1,0:T(8,128)(2,1)}, u32[]{:S(2)}, u32[]{:S(2)}) collective-permute-start(bf16[128,768]{1,0:T(8,128)(2,1)} %slice.52), channel_id=1, source_target_pairs={{0,8},{8,16},{16,24},{1,9},{9,17},{17,25},{2,10},{10,18},{18,26},{... | collective-permute-start | bytes 589832 | tf_op jit(solution)/shard_map/ppermute | solution.py:21
Sparse Core Ops, SparseCore 0:
  19.9 27.4 all-gather.1
where the time goes:
time: 218 us; the launch traced here: 217 us
  local copies, waits for them, and re-layouts  74.2 us (34%)
  blocking collectives  42.4 us (19%)
  matrix products  31.7 us (15%)
  other arithmetic  28.2 us (13%)
  between operations  13.7 us (6%)
  starting transfers between devices  11.9 us (5%)
  loops' own time  7.63 us (4%)
  waiting for transfers between devices  7.09 us (3%)
    all_gather x1, blocking collectives, shards(): lax.all_gather(local_summary, ('grp', 'seq'), axis=1, tiled=True)  42.4 us
    dot_general x12, matrix products, attend(): jnp.einsum('bghtn,bgnd->bghtd', rounded, key_block[..., head_dim:], prefe...  17.7 us
    another operation x2, local copies, waits for them, and re-layouts, shards(): by_heads(query_blocks, chosen, allowed_sel, False)  17.5 us
    dot_general x12, matrix products, attend(): jnp.einsum('btghd,bgnd->bghtn', query_block, key_block[..., :head_dim], p...  13.8 us
    dynamic_slice x12, local copies, waits for them, and re-layouts, by_heads(): lax.map(head_slab, jnp.arange(head_count // slab_width, dtype=jnp.int32))  9.99 us
    sub x4, other arithmetic, attend(): weights = jnp.where(allowed_wide, jnp.exp(scores - top_score), 0.0)  8.59 us
    another operation x3, loops' own time, by_heads(): lax.map(head_slab, jnp.arange(head_count // slab_width, dtype=jnp.int32))  7.63 us
    all_to_all x1, waiting for transfers between devices, shards(): lax.all_to_all(local_view[asked_clipped % dev_blocks, :, asked_clipped //...  6.38 us
  transfers between devices with their start and end apart: 4, of which 1 were waited for; matrix products, arithmetic and copies ran while one was open for 37% of the time, Pallas kernels for 0%

commit v1 on v0

--- a/solution.py
+++ b/solution.py
@@ -13,6 +13,18 @@
 CAP = 2
 WINDOW = 128
 NEG_FILL = -1e30
+
+
+def doubled_up(shard, axis, dim):
+    ways, here, step = (lax.axis_size(axis), lax.axis_index(axis), shard.shape[dim])
+    line, have = (shard, 1)
+    while have < ways:
+        line = jnp.concatenate(
+            [line, lax.ppermute(line, axis, [(d, (d - have) % ways) for d in range(ways)])],
+            axis=dim,
+        )
+        have = 2 * have
+    return jnp.roll(line, here * step, axis=dim)
 
 
 def from_behind(block, axis, distance):
@@ -120,7 +132,7 @@
     local_summary = jnp.transpose(
         compress_blocks(keys_values, pos_weight, compress_weight), (1, 0, 2)
     )
-    summaries = lax.all_gather(local_summary, ("grp", "seq"), axis=1, tiled=True)
+    summaries = doubled_up(local_summary, ("grp", "seq"), 1)
     picked = selection.reshape(dev_blocks, GROUPS, TOP)
     group_ids = jnp.broadcast_to(jnp.arange(GROUPS, dtype=jnp.int32)[None, :, None], picked.shape)
     flat_groups = group_ids.reshape(-1)

time: 218 us -> 182 us (0.83)
  the two profiles are of different devices: /device:TPU:0 before, /device:TPU:6 now
where the time goes in v1:
time: 182 us; the launch traced here: 180 us
  local copies, waits for them, and re-layouts  63.9 us (35%)
  matrix products  31.2 us (17%)
  other arithmetic  28.1 us (15%)
  starting transfers between devices  26.1 us (14%)
  between operations  13.7 us (8%)
  waiting for transfers between devices  9.57 us (5%)
  loops' own time  7.43 us (4%)
    dot_general x12, matrix products, attend(): jnp.einsum('bghtn,bgnd->bghtd', rounded, key_block[..., head_dim:], prefe...  21.3 us
    another operation x2, local copies, waits for them, and re-layouts, shards(): by_heads(query_blocks, chosen, allowed_sel, False)  17.5 us
    ppermute x5, starting transfers between devices, doubled_up(): lax.ppermute(line, axis, [(d, (d - have) % ways) for d in range(ways)])  11.4 us
    dot_general x12, matrix products, attend(): jnp.einsum('btghd,bgnd->bghtn', query_block, key_block[..., :head_dim], p...  9.82 us
    ppermute x5, waiting for transfers between devices, doubled_up(): lax.ppermute(line, axis, [(d, (d - have) % ways) for d in range(ways)])  8.85 us
    sub x4, other arithmetic, attend(): weights = jnp.where(allowed_wide, jnp.exp(scores - top_score), 0.0)  8.59 us
    another operation x3, loops' own time, by_heads(): lax.map(head_slab, jnp.arange(head_count // slab_width, dtype=jnp.int32))  7.43 us
    dynamic_slice x12, local copies, waits for them, and re-layouts, by_heads(): lax.map(head_slab, jnp.arange(head_count // slab_width, dtype=jnp.int32))  6.96 us
  transfers between devices with their start and end apart: 9, of which 3 were waited for; matrix products, arithmetic and copies ran while one was open for 39% of the time, Pallas kernels for 0%

profile of v1, /device:TPU:6, one launch (start us, length us, event | category | flops | bytes accessed | tf_op | source)
XLA Modules:
  0.0 180.0 jit_solution(8192941719297254235)
XLA Ops:
  9.7 4.9 %all-to-all-start = ((s32[4,1,2]{2,1,0:T(1,128)}), s32[4,1,2]{2,1,0:T(1,128)S(1)}, u32[]{:S(2)}, u32[]{:S(2)}) async-start(s32[4,1,2]{2,1,0:T(1,128)} %copy.101), calls=%async_computation | async-start | bytes 4096 | tf_op jit(solution)/shard_map/all_to_all | solution.py:146
  19.5 3.4 %reshape.537 = bf16[2,64,2,16,192]{4,3,2,1,0:T(8,128)(2,1)} reshape(bf16[128,6144]{1,0:T(8,128)(2,1)S(1)} %copy-done.2) | data formatting | bytes 3145728 | tf_op jit(solution)/shard_map/reshape | solution.py:177
  26.7 4.3 %collective-permute-done.1 = bf16[2,4,384]{2,0,1:T(2,128)(2,1)S(1)} collective-permute-done((bf16[2,4,384]{2,0,1:T(2,128)(2,1)S(1)}, bf16[2,4,384]{2,0,1:T(2,128)(2,1)S(1)}, u32[]{:S(2)}, u32[]{:S(2)}) %collective-permute-start.1) | collective-permute-done | bytes 6176 | tf_op jit(solution)/shard_map/ppermute | solution.py:23
  32.6 3.0 %collective-permute-done.2 = bf16[2,8,384]{2,0,1:T(2,128)(2,1)S(1)} collective-permute-done((bf16[2,8,384]{2,0,1:T(2,128)(2,1)S(1)}, bf16[2,8,384]{2,0,1:T(2,128)(2,1)S(1)}, u32[]{:S(2)}, u32[]{:S(2)}) %collective-permute-start.2) | collective-permute-done | bytes 12320 | tf_op jit(solution)/shard_map/ppermute | solution.py:23
  35.7 7.7 %collective-permute-start.3 = (bf16[2,16,384]{2,0,1:T(2,128)(2,1)S(1)}, bf16[2,16,384]{2,0,1:T(2,128)(2,1)S(1)}, u32[]{:S(2)}, u32[]{:S(2)}) collective-permute-start(bf16[2,16,384]{2,0,1:T(2,128)(2,1)S(1)} %pad_maximum_fusion.1), channel_id=1, source_target_pairs={{0,24},{1,25},{2,26},{3,27},{4,28},{5,29},{6,30},{7,31},{8,0},{9,1... | collective-permute-start | bytes 73736 | tf_op jit(solution)/shard_map/ppermute | solution.py:23
  47.4 5.1 %all-to-all-start.1 = ((bf16[4,2,64,384]{3,2,1,0:T(8,128)(2,1)}), bf16[4,2,64,384]{3,2,1,0:T(8,128)(2,1)S(1)}, u32[]{:S(2)}, u32[]{:S(2)}) async-start(bf16[4,2,64,384]{3,2,1,0:T(8,128)(2,1)} %bitcast.14), calls=%async_computation.1 | async-start | bytes 786432 | tf_op jit(solution)/shard_map/all_to_all | solution.py:148
  55.0 11.8 %while.33 = (s32[]{:T(128)}, f32[4,1,128,2,4,192]{2,5,4,0,3,1:T(8,128)}, s32[4]{0:T(128)S(1)}, bf16[1,128,2,16,192]{1,4,3,2,0:T(8,128)(2,1)S(1)}, bf16[1,2,64,38...) while((s32[]{:T(128)}, ...), condition=%wide.region_4.5_spmd.clone, body=%wide.region_1.4_spmd.clone.sunk | while | flops 51128324 | bytes 2172331 | solution.py:78
  66.8 2.7 %gather_fusion.2 = bf16[64,64,384]{2,1,0:T(8,128)(2,1)} fusion(bf16[4,2,64,384]{3,2,1,0:T(8,128)(2,1)S(1)} %all-to-all-done.1, s32[64]{0:T(128)S(1)} %reshape.553), kind=kCustom, calls=%fused_computation.2 | custom fusion | bytes 6291968 | tf_op jit(solution)/shard_map/gather | solution.py:157
  69.5 3.4 %reshape.538 = bf16[16,64,2,384]{3,2,1,0:T(2,128)(2,1)S(1)} reshape(bf16[1024,768]{1,0:T(8,128)(2,1)} %all-gather.2.cloned.1.call-done) | data formatting | bytes 3145728 | tf_op jit(solution)/shard_map/reshape | solution.py:160
  73.2 2.7 %gather_fusion = bf16[64,64,384]{2,1,0:T(8,128)(2,1)} fusion(bf16[16,64,2,384]{3,1,2,0:T(8,128)(2,1)S(1)} %copy.100, s32[64]{0:T(128)S(1)} %reshape.541), kind=kCustom, calls=%fused_computation | custom fusion | bytes 6291968 | tf_op jit(solution)/shard_map/gather | solution.py:161
  75.9 4.4 %broadcast_select_fusion = bf16[2,2,1024,384]{3,2,1,0:T(8,128)(2,1)} fusion(bf16[2,2,1024,384]{3,2,1,0:T(8,128)(2,1)} %bitcast.258, bf16[2,2,1024,384]{3,2,1,0:T(8,128)(2,1)} %bitcast.257, pred[2,2,1024]{2,1,0:T(4,128)(4,1)S(1)} %broadcast_in_dim.161), kind=kLoop, calls=%fused_computation.84 | loop fusion | flops 1572864 | bytes 9441280 | tf_op jit(solution)/shard_map/jit(_where)/select_n | solution.py:166
  80.2 3.2 %copy.108 = bf16[2,2,1024,384]{2,3,1,0:T(8,128)(2,1)S(1)} copy(bf16[2,2,1024,384]{3,2,1,0:T(8,128)(2,1)} %broadcast_select_fusion) | data formatting | bytes 6291456
  85.0 4.8 %collective-permute-start.5 = (bf16[128,768]{1,0:T(8,128)(2,1)}, bf16[128,768]{1,0:T(8,128)(2,1)}, u32[]{:S(2)}, u32[]{:S(2)}) collective-permute-start(bf16[128,768]{1,0:T(8,128)(2,1)} %slice.52), channel_id=1, source_target_pairs={{0,8},{8,16},{16,24},{1,9},{9,17},{17,25},{2,10},{10,18},{18,26},{... | collective-permute-start | bytes 589832 | tf_op jit(solution)/shard_map/ppermute | solution.py:33
  89.8 30.0 %while.34 = (s32[]{:T(128)}, f32[4,2,64,2,4,192]{5,2,4,3,1,0:T(8,128)}, s32[4]{0:T(128)S(1)}, bf16[2,64,2,16,192]{4,3,2,1,0:T(8,128)(2,1)}, bf16[2,2,1024,384]{2...) while((s32[]{:T(128)}, ...), condition=%wide.region_12.13_spmd.clone, body=%wide.region_9.12_spmd.clone.sunk | while | flops 814416896 | bytes 18646196 | solution.py:78
  101.0 2.1 %fusion.132 = (f32[2,2,4,64]{3,2,1,0:T(4,128)S(1)}, bf16[2,2,4,64,1024]{4,3,2,1,0:T(8,128)(2,1)S(1)}) fusion(f32[2,2,64,4,1024]{4,2,3,1,0:T(8,128)S(1)} %fusion.131, pred[2,2,64,1024]{3,2,1,0:T(8,128)(4,1)S(1)} %compare_and_fusion.4), kind=kOutput, calls=%fused_computation.166.clone.1 | output fusion | flops 8389631 | bytes 6557696 | tf_op jit(solution)/shard_map/while/body/eval_jaxpr/sub | solution.py:53
  119.9 11.7 %copy.121 = f32[2,64,2,4,4,192]{1,0,5,4,3,2:T(2,128)} copy(f32[2,64,2,4,4,192]{5,1,4,2,0,3:T(8,128)} %bitcast.16) | data formatting | bytes 6291456 | tf_op jit(solution)/shard_map/reshape;reshape | solution.py:178
  131.6 5.8 %reshape.575 = f32[128,6144]{0,1:T(8,128)S(1)} reshape(f32[2,64,2,4,4,192]{1,0,5,4,3,2:T(2,128)} %copy.121) | data formatting | bytes 6291456 | tf_op jit(solution)/shard_map/reshape;reshape | solution.py:178
  144.1 21.9 %while.35 = (s32[]{:T(128)}, f32[4,1,128,2,4,192]{2,5,4,0,3,1:T(8,128)}, s32[4]{0:T(128)S(1)}, bf16[1,128,2,16,192]{1,4,3,2,0:T(8,128)(2,1)}, bf16[1,2,256,384]{...) while((s32[]{:T(128)}, ...), condition=%wide.region_16.17_spmd.clone, body=%wide.region_13.16_spmd.clone.sunk | while | flops 204011520 | bytes 4873147 | solution.py:78
  147.3 2.2 %fusion.138 = f32[4,1,128,2,4,192]{2,5,4,0,3,1:T(8,128)} fusion(f32[4,1,128,2,4,192]{2,5,4,0,3,1:T(8,128)} %get-tuple-element.472, s32[]{:T(128)} %get-tuple-element.471, f32[1,2,4,128,256]{4,3,2,1,0:T(8,128)S(1)} %get-tuple-element.456, f32[2,4,128]{2,1,0:T(4,128)S(1)} %get-tuple-element.457, pred[128,256]{1,0:T(8,128)(4,1)S(1)} %and_and_fusion.2, ...), kind=kOutput, calls=%fused_computation.60.clone.1 | convolution fusion | flops 101646336 | bytes 2073088 | tf_op jit(solution)/shard_map/while/body/eval_jaxpr/bghtn,bgnd->bghtd/dot_general | solution.py:59
  152.8 2.3 %fusion.138 = f32[4,1,128,2,4,192]{2,5,4,0,3,1:T(8,128)} fusion(f32[4,1,128,2,4,192]{2,5,4,0,3,1:T(8,128)} %get-tuple-element.472, s32[]{:T(128)} %get-tuple-element.471, f32[1,2,4,128,256]{4,3,2,1,0:T(8,128)S(1)} %get-tuple-element.456, f32[2,4,128]{2,1,0:T(4,128)S(1)} %get-tuple-element.457, pred[128,256]{1,0:T(8,128)(4,1)S(1)} %and_and_fusion.2, ...), kind=kOutput, calls=%fused_computation.60.clone.1 | convolution fusion | flops 101646336 | bytes 2073088 | tf_op jit(solution)/shard_map/while/body/eval_jaxpr/bghtn,bgnd->bghtd/dot_general | solution.py:59
  158.2 2.2 %fusion.138 = f32[4,1,128,2,4,192]{2,5,4,0,3,1:T(8,128)} fusion(f32[4,1,128,2,4,192]{2,5,4,0,3,1:T(8,128)} %get-tuple-element.472, s32[]{:T(128)} %get-tuple-element.471, f32[1,2,4,128,256]{4,3,2,1,0:T(8,128)S(1)} %get-tuple-element.456, f32[2,4,128]{2,1,0:T(4,128)S(1)} %get-tuple-element.457, pred[128,256]{1,0:T(8,128)(4,1)S(1)} %and_and_fusion.2, ...), kind=kOutput, calls=%fused_computation.60.clone.1 | convolution fusion | flops 101646336 | bytes 2073088 | tf_op jit(solution)/shard_map/while/body/eval_jaxpr/bghtn,bgnd->bghtd/dot_general | solution.py:59
  163.7 2.3 %fusion.138 = f32[4,1,128,2,4,192]{2,5,4,0,3,1:T(8,128)} fusion(f32[4,1,128,2,4,192]{2,5,4,0,3,1:T(8,128)} %get-tuple-element.472, s32[]{:T(128)} %get-tuple-element.471, f32[1,2,4,128,256]{4,3,2,1,0:T(8,128)S(1)} %get-tuple-element.456, f32[2,4,128]{2,1,0:T(4,128)S(1)} %get-tuple-element.457, pred[128,256]{1,0:T(8,128)(4,1)S(1)} %and_and_fusion.2, ...), kind=kOutput, calls=%fused_computation.60.clone.1 | convolution fusion | flops 101646336 | bytes 2073088 | tf_op jit(solution)/shard_map/while/body/eval_jaxpr/bghtn,bgnd->bghtd/dot_general | solution.py:59
  166.0 4.6 %fusion.84 = bf16[128,6144]{0,1:T(8,128)(2,1)} fusion(f32[4,1,128,2,4,192]{2,5,4,0,3,1:T(8,128)} %get-tuple-element.103, f32[4,1,128,2,4,192]{2,5,4,0,3,1:T(8,128)} %get-tuple-element.101, f32[128,6144]{0,1:T(8,128)S(1)} %reshape.575, f32[128,2,16]{0,2,1:T(8,128)S(1)} %bitcast.267, f32[128,2,16]{0,2,1:T(8,128)S(1)} %bitcast.268, f32[128,2,16]{0,2,1:T(8,128)S(1)} %bitcast.266), kind=kLoop, calls=%fused_computation.80 | loop fusion | flops 4718592 | bytes 11059200 | tf_op jit(solution)/shard_map/convert_element_type | solution.py:204
  170.6 2.6 %copy.113 = bf16[128,6144]{1,0:T(8,128)(2,1)} copy(bf16[128,6144]{0,1:T(8,128)(2,1)} %fusion.84) | data formatting | bytes 3145728 | tf_op jit(solution)/shard_map/convert_element_type | solution.py:204
  (175 shorter events, 73.5 us)
Async XLA Ops:
  6.5 10.8 %copy-start = (bf16[384,384]{1,0:T(8,128)(2,1)S(1)}, bf16[384,384]{1,0:T(8,128)(2,1)}, u32[]{:S(2)}) copy-start(bf16[384,384]{1,0:T(8,128)(2,1)} %param.17) | copy-start | bytes 884740
  6.5 13.0 %copy-start.2 = (bf16[128,6144]{1,0:T(8,128)(2,1)S(1)}, bf16[128,6144]{1,0:T(8,128)(2,1)}, u32[]{:S(2)}) copy-start(bf16[128,6144]{1,0:T(8,128)(2,1)} %param.12) | copy-start | bytes 4718596
  9.7 15.7 %all-to-all-start = ((s32[4,1,2]{2,1,0:T(1,128)}), s32[4,1,2]{2,1,0:T(1,128)S(1)}, u32[]{:S(2)}, u32[]{:S(2)}) async-start(s32[4,1,2]{2,1,0:T(1,128)} %copy.101), calls=%async_computation | async-start | bytes 4096 | tf_op jit(solution)/shard_map/all_to_all | solution.py:146
  14.6 54.9 %all-gather.2.cloned.1.call-start = ((), (), s32[]{:S(2)}) async-start(), calls=%async_computation.2 | async-start | bytes 1769472 | tf_op jit(solution)/shard_map/all_gather | solution.py:158
  17.5 8.0 %collective-permute-start = (bf16[2,2,384]{2,0,1:T(2,128)(2,1)S(1)}, bf16[2,2,384]{2,0,1:T(2,128)(2,1)S(1)}, u32[]{:S(2)}, u32[]{:S(2)}) collective-permute-start(bf16[2,2,384]{2,0,1:T(2,128)(2,1)S(1)} %bitcast.262), channel_id=1, source_target_pairs={{0,31},{1,0},{2,1},{3,2},{4,3},{5,4},{6,5},{7,6},{8,7},{9,8},{10,9... | collective-permute-start | bytes 9224 | tf_op jit(solution)/shard_map/ppermute | solution.py:23
  25.5 5.5 %collective-permute-start.1 = (bf16[2,4,384]{2,0,1:T(2,128)(2,1)S(1)}, bf16[2,4,384]{2,0,1:T(2,128)(2,1)S(1)}, u32[]{:S(2)}, u32[]{:S(2)}) collective-permute-start(bf16[2,4,384]{2,0,1:T(2,128)(2,1)S(1)} %pad_maximum_fusion.3), channel_id=1, source_target_pairs={{0,30},{1,31},{2,0},{3,1},{4,2},{5,3},{6,4},{7,5},{8,6},{9,7},{10,... | collective-permute-start | bytes 18440 | tf_op jit(solution)/shard_map/ppermute | solution.py:23
  31.0 4.6 %collective-permute-start.2 = (bf16[2,8,384]{2,0,1:T(2,128)(2,1)S(1)}, bf16[2,8,384]{2,0,1:T(2,128)(2,1)S(1)}, u32[]{:S(2)}, u32[]{:S(2)}) collective-permute-start(bf16[2,8,384]{2,0,1:T(2,128)(2,1)S(1)} %pad_maximum_fusion.2), channel_id=1, source_target_pairs={{0,28},{1,29},{2,30},{3,31},{4,0},{5,1},{6,2},{7,3},{8,4},{9,5},{1... | collective-permute-start | bytes 36872 | tf_op jit(solution)/shard_map/ppermute | solution.py:23
  35.7 9.2 %collective-permute-start.3 = (bf16[2,16,384]{2,0,1:T(2,128)(2,1)S(1)}, bf16[2,16,384]{2,0,1:T(2,128)(2,1)S(1)}, u32[]{:S(2)}, u32[]{:S(2)}) collective-permute-start(bf16[2,16,384]{2,0,1:T(2,128)(2,1)S(1)} %pad_maximum_fusion.1), channel_id=1, source_target_pairs={{0,24},{1,25},{2,26},{3,27},{4,28},{5,29},{6,30},{7,31},{8,0},{9,1... | collective-permute-start | bytes 73736 | tf_op jit(solution)/shard_map/ppermute | solution.py:23
  45.0 7.6 %collective-permute-start.4 = (bf16[2,32,384]{2,0,1:T(2,128)(2,1)S(1)}, bf16[2,32,384]{2,0,1:T(2,128)(2,1)S(1)}, u32[]{:S(2)}, u32[]{:S(2)}) collective-permute-start(bf16[2,32,384]{2,0,1:T(2,128)(2,1)S(1)} %get-tuple-element.276), channel_id=1, source_target_pairs={{0,16},{1,17},{2,18},{3,19},{4,20},{5,21},{6,22},{7,23},{8,24},{9,... | collective-permute-start | bytes 147464 | tf_op jit(solution)/shard_map/ppermute | solution.py:23
  47.4 19.4 %all-to-all-start.1 = ((bf16[4,2,64,384]{3,2,1,0:T(8,128)(2,1)}), bf16[4,2,64,384]{3,2,1,0:T(8,128)(2,1)S(1)}, u32[]{:S(2)}, u32[]{:S(2)}) async-start(bf16[4,2,64,384]{3,2,1,0:T(8,128)(2,1)} %bitcast.14), calls=%async_computation.1 | async-start | bytes 786432 | tf_op jit(solution)/shard_map/all_to_all | solution.py:148
  66.8 2.7 %copy-start.1 = (bf16[1,128,2,16,192]{1,4,3,2,0:T(8,128)(2,1)}, bf16[1,128,2,16,192]{1,4,3,2,0:T(8,128)(2,1)S(1)}, u32[]{:S(2)}) copy-start(bf16[1,128,2,16,192]{1,4,3,2,0:T(8,128)(2,1)S(1)} %get-tuple-element.568) | copy-start | bytes 4718596
  85.0 52.4 %collective-permute-start.5 = (bf16[128,768]{1,0:T(8,128)(2,1)}, bf16[128,768]{1,0:T(8,128)(2,1)}, u32[]{:S(2)}, u32[]{:S(2)}) collective-permute-start(bf16[128,768]{1,0:T(8,128)(2,1)} %slice.52), channel_id=1, source_target_pairs={{0,8},{8,16},{16,24},{1,9},{9,17},{17,25},{2,10},{10,18},{18,26},{... | collective-permute-start | bytes 589832 | tf_op jit(solution)/shard_map/ppermute | solution.py:33
Sparse Core Ops, SparseCore 0:
  17.3 26.2 all-gather.1
